TPU v7x, 512 devices: a whole 4x4x16 slice. The times are simulated.
512 devices in a mesh: row: 32 (over z, core), col: 16 (over x, y).
Axes of the slice: x: 4, y: 4, z: 16, core: 2. Of those that a mesh axis runs over, the one named last changes fastest.
Arguments:
- matrix: float32 [8192, 8192], P('row', 'col'), may hold values from -6 to 6
- pivots: int32 [3, 256], replicated, may hold values from 0 to 8191, as said below
- inverses: float32 [3, 256, 256], replicated, may hold values from -0.0234375 to 0.0234375
Outputs:
- factored: float32 [8192, 8192], P('row', 'col')
Inputs may be any that keep to these rules, and one draw needn't show every extreme that they name: For panel k and position i, pivots[k, i] is either k * 256 + i or a row of index (k + 1) * 256 or more; position 0 of every panel is k * 256; no row is named twice within one panel; every panel names row 8191.
All inputs are finite; a program needn't handle non-finite values.
Results may differ from a plain program's by a relative error of at most 0.00017.
Values sent between devices are 32-bit elements; how exact they have to be, the bound alone decides.
A program may use at most 64 MiB of HBM per device.

v0:
```python
import jax
import jax.numpy as jnp
from jax import lax
from jax.sharding import PartitionSpec as P


def broadcast(array, axis, root):
    mine = lax.axis_index(axis) == root
    return lax.psum(jnp.where(mine, array, jnp.zeros_like(array)), axis)


def on_device(matrix, pivots, inverses):
    rows_here, cols_here = matrix.shape
    block = inverses.shape[1]
    nrow = lax.axis_size("row")
    ncol = lax.axis_size("col")
    rank_row = lax.axis_index("row")
    rank_col = lax.axis_index("col")
    local_rows = jnp.arange(rows_here, dtype=jnp.int32)
    global_rows = (local_rows // block * nrow + rank_row) * block + local_rows % block
    col_index = jnp.arange(cols_here, dtype=jnp.int32)
    global_cblock = col_index // block * ncol + rank_col
    offsets = jnp.arange(block, dtype=jnp.int32)
    current = matrix
    for panel in range(pivots.shape[0]):
        top = panel * block
        chosen = pivots[panel]
        stay = chosen == top + offsets
        owner = chosen // block % nrow
        local_pick = chosen // block // nrow * block + chosen % block
        local_pick = jnp.clip(local_pick, 0, rows_here - 1)
        picked = jnp.where((owner == rank_row)[:, None], current[local_pick], 0.0)
        diag_owner = panel % nrow
        diag_local = panel // nrow * block
        diag_block = current
        upper = lax.psum(picked, "row")
        displaced = broadcast(diag_block, "row", diag_owner)
        matches = (global_rows[:, None] == chosen[None, :]) & jnp.logical_not(stay)[None, :]
        has_match = jnp.any(matches, axis=1)
        source = jnp.sum(jnp.where(matches, offsets[None, :], 0), axis=1)
        in_diag = (global_rows >= top) & (global_rows < top + block)
        diag_pos = jnp.clip(global_rows - top, 0, block - 1)
        swapped = jnp.where(
            has_match[:, None],
            displaced[source],
            jnp.where(in_diag[:, None], upper[diag_pos], current),
        )
        col_owner = panel % ncol
        col_local = panel // ncol * block
        strip = swapped[:, col_local : col_local + block]
        below = (global_rows >= top + block)[:, None]
        made = jnp.where(
            below,
            jnp.dot(
                strip,
                inverses[panel],
                precision=lax.Precision.HIGHEST,
                preferred_element_type=jnp.float32,
            ),
            0.0,
        )
        factor = broadcast(made, "col", col_owner)
        replaced = jnp.where(below & (rank_col == col_owner), factor, strip)
        swapped = swapped.at[:, col_local : col_local + block].set(replaced)
        update = jnp.dot(
            factor, upper, precision=lax.Precision.HIGHEST, preferred_element_type=jnp.float32
        )
        current = swapped - jnp.where((global_cblock > panel)[None, :], update, 0.0)
    return current


def solution(mesh):
    placed = (P("row", "col"), P(), P())
    return jax.shard_map(
        on_device, mesh=mesh, in_specs=placed, out_specs=P("row", "col"), check_vma=False
    )
```

profile of v0, /device:TPU:2, one launch (start us, length us, event | category | flops | bytes accessed | tf_op | source)
XLA Modules:
  0.0 1026.0 jit_solution(13716612972238767918)
XLA Ops:
  6.5 0.8 fusion.45
  7.4 0.3 select_reduce_fusion
  7.8 1.9 broadcast_select_fusion.5
  9.8 1.0 gather_fusion.1
  10.7 0.9 broadcast_select_fusion.4
  12.1 213.8 %all-reduce.20.cloned.1.call-done = (f32[256,512]{1,0:T(8,128)}, f32[256,512]{1,0:T(8,128)}) async-done(((f32[256,512]{1,0:T(8,128)}, f32[256,512]{1,0:T(8,128)}), (f32[256,512]{1,0:T(8,128)}, f32[256,512]{1,0:T(8,128)})) %all-reduce.20.cloned.1.call-update) | async-done | bytes 1048592 | tf_op jit(solution)/shard_map/psum | solution.py:9
  225.9 2.3 gather_fusion
  228.2 1.0 gather_fusion.2
  229.4 1.0 copy-done.7
  230.3 1.1 fusion.5
  231.5 0.7 compare_reduce_fusion
  232.2 114.0 %all-reduce.10.cloned.1.call-done = f32[256,256]{1,0:T(8,128)} async-done(((f32[256,256]{1,0:T(8,128)}), f32[256,256]{1,0:T(8,128)}) %all-reduce.10.cloned.1.call-update) | async-done | bytes 262160 | tf_op jit(solution)/shard_map/psum | solution.py:9
  346.2 1.7 fusion.6
  347.9 1.5 broadcast_select_fusion.3
  349.4 1.0 gather_fusion.4
  350.4 0.9 broadcast_select_fusion.2
  351.5 210.3 %all-reduce.18.cloned.1.call-done = (f32[256,512]{1,0:T(8,128)}, f32[256,512]{1,0:T(8,128)}) async-done(((f32[256,512]{1,0:T(8,128)}, f32[256,512]{1,0:T(8,128)}), (f32[256,512]{1,0:T(8,128)}, f32[256,512]{1,0:T(8,128)})) %all-reduce.18.cloned.1.call-update) | async-done | bytes 1048592 | tf_op jit(solution)/shard_map/psum | solution.py:9
  561.8 2.3 gather_fusion.3
  564.1 1.0 gather_fusion.5
  565.2 1.1 fusion.4
  566.4 114.7 %all-reduce.12.cloned.1.call-done = f32[256,256]{1,0:T(8,128)} async-done(((f32[256,256]{1,0:T(8,128)}), f32[256,256]{1,0:T(8,128)}) %all-reduce.12.cloned.1.call-update) | async-done | bytes 262160 | tf_op jit(solution)/shard_map/psum | solution.py:9
  681.1 1.7 fusion.7
  682.8 1.5 broadcast_select_fusion.1
  684.3 1.0 gather_fusion.7
  685.3 0.9 broadcast_select_fusion
  686.3 210.3 %all-reduce.16.cloned.1.call-done = (f32[256,512]{1,0:T(8,128)}, f32[256,512]{1,0:T(8,128)}) async-done(((f32[256,512]{1,0:T(8,128)}, f32[256,512]{1,0:T(8,128)}), (f32[256,512]{1,0:T(8,128)}, f32[256,512]{1,0:T(8,128)})) %all-reduce.16.cloned.1.call-update) | async-done | bytes 1048592 | tf_op jit(solution)/shard_map/psum | solution.py:9
  896.7 2.3 gather_fusion.6
  899.0 1.0 gather_fusion.8
  900.1 1.1 fusion.3
  901.3 114.7 %all-reduce.14.cloned.1.call-done = f32[256,256]{1,0:T(8,128)} async-done(((f32[256,256]{1,0:T(8,128)}), f32[256,256]{1,0:T(8,128)}) %all-reduce.14.cloned.1.call-update) | async-done | bytes 262160 | tf_op jit(solution)/shard_map/psum | solution.py:9
  1016.0 1.7 fusion.8
  1017.7 1.4 fusion
  (59 shorter events, 1.4 us)
Async XLA Ops:
  6.5 0.8 copy-start.8
  6.5 219.4 %all-reduce.20.cloned.1.call-start = ((), (), s32[]{:S(2)}) async-start(), calls=%async_computation.5 | async-start | bytes 2097152 | tf_op jit(solution)/shard_map/psum | solution.py:9
  7.8 2.0 copy-start
  11.7 334.5 %all-reduce.10.cloned.1.call-start = ((), (), s32[]{:S(2)}) async-start(), calls=%async_computation | async-start | bytes 524288 | tf_op jit(solution)/shard_map/psum | solution.py:9
  225.9 2.3 copy-start.1
  229.2 1.1 copy-start.7
  231.5 330.3 %all-reduce.18.cloned.1.call-start = ((), (), s32[]{:S(2)}) async-start(), calls=%async_computation.4 | async-start | bytes 2097152 | tf_op jit(solution)/shard_map/psum | solution.py:9
  346.2 1.7 copy-start.4
  351.3 329.8 %all-reduce.12.cloned.1.call-start = ((), (), s32[]{:S(2)}) async-start(), calls=%async_computation.1 | async-start | bytes 524288 | tf_op jit(solution)/shard_map/psum | solution.py:9
  561.8 2.3 copy-start.2
  566.4 330.3 %all-reduce.16.cloned.1.call-start = ((), (), s32[]{:S(2)}) async-start(), calls=%async_computation.3 | async-start | bytes 2097152 | tf_op jit(solution)/shard_map/psum | solution.py:9
  681.1 1.7 copy-start.5
  686.2 329.8 %all-reduce.14.cloned.1.call-start = ((), (), s32[]{:S(2)}) async-start(), calls=%async_computation.2 | async-start | bytes 524288 | tf_op jit(solution)/shard_map/psum | solution.py:9
  896.7 2.3 copy-start.3
  1016.0 1.7 copy-start.6
Sparse Core Ops, SparseCore 0:
  11.8 214.0 all-reduce.19
  231.6 114.5 all-reduce.9
  351.4 210.2 all-reduce.17
  566.5 114.5 all-reduce.11
  686.3 210.2 all-reduce.15
  901.4 114.5 all-reduce.13
where the time goes:
time: 1030 us
  waiting for transfers between devices  978 us (95%)
  local copies, waits for them, and re-layouts  14.6 us (1%)
  between operations  13.8 us (1%)
  other arithmetic  11.8 us (1%)
    psum x6, waiting for transfers between devices, broadcast(): return lax.psum(jnp.where(mine, array, jnp.zeros_like(array)), axis)  978 us
  transfers between devices with their start and end apart: 6, of which 6 were waited for; matrix products, arithmetic and copies ran while one was open for 0% of the time, Pallas kernels for 0%

commit v1 on v0

--- a/solution.py
+++ b/solution.py
@@ -6,7 +6,7 @@
 
 def broadcast(array, axis, root):
     mine = lax.axis_index(axis) == root
-    return lax.psum(jnp.where(mine, array, jnp.zeros_like(array)), axis)
+    return jnp.sum(lax.all_gather(jnp.where(mine, array, jnp.zeros_like(array)), axis), axis=0)
 
 
 def on_device(matrix, pivots, inverses):

time: 1030 us -> 1220 us (1.18)
  the two profiles are of different devices: /device:TPU:2 before, /device:TPU:1 now
where the time goes in v1:
time: 1220 us
  waiting for transfers between devices  1140 us (93%)
  other arithmetic  39.9 us (3%)
  local copies, waits for them, and re-layouts  15 us (1%)
  between operations  13.5 us (1%)
    psum x3, waiting for transfers between devices, on_device(): upper = lax.psum(picked, 'row')  626 us
    all_gather x6, waiting for transfers between devices, broadcast(): lax.all_gather(jnp.where(mine, array, jnp.zeros_like(array)), axis)  513 us
    reduce_sum x6, other arithmetic, broadcast(): jnp.sum(lax.all_gather(jnp.where(mine, array, jnp.zeros_like(array)), axi...  30.7 us
  transfers between devices with their start and end apart: 9, of which 9 were waited for; matrix products, arithmetic and copies ran while one was open for 1% of the time, Pallas kernels for 0%

profile of v1, /device:TPU:1, one launch (start us, length us, event | category | flops | bytes accessed | tf_op | source)
XLA Modules:
  0.0 1216.9 jit_solution(3141198002231229392)
XLA Ops:
  9.4 2.3 gather_fusion.1
  11.7 0.9 broadcast_select_fusion.4
  14.0 212.1 %all-reduce.4.cloned.1.call-done = f32[256,512]{1,0:T(8,128)} async-done(((f32[256,512]{1,0:T(8,128)}), f32[256,512]{1,0:T(8,128)}) %all-reduce.4.cloned.1.call-update) | async-done | bytes 524304 | tf_op jit(solution)/shard_map/psum | solution.py:36
  226.1 2.3 gather_fusion.2
  228.4 106.9 %all-gather.13.cloned.1.call-done = f32[8192,512]{1,0:T(8,128)} async-done(((f32[256,512]{1,0:T(8,128)}), f32[8192,512]{1,0:T(8,128)}) %all-gather.13.cloned.1.call-update) | async-done | bytes 16777232 | tf_op jit(solution)/shard_map/all_gather | solution.py:9
  335.4 7.8 reduce_sum.87
  343.1 1.0 gather_fusion
  344.3 1.1 fusion.5
  346.1 63.7 %all-gather.15.cloned.1.call-done = f32[4096,256]{1,0:T(8,128)} async-done(((f32[256,256]{1,0:T(8,128)}), f32[4096,256]{1,0:T(8,128)}) %all-gather.15.cloned.1.call-update) | async-done | bytes 4194320 | tf_op jit(solution)/shard_map/all_gather | solution.py:9
  409.8 2.5 reduce_sum.90
  413.0 1.5 broadcast_select_fusion.3
  414.4 1.0 gather_fusion.4
  417.1 207.2 %all-reduce.6.cloned.1.call-done = f32[256,512]{1,0:T(8,128)} async-done(((f32[256,512]{1,0:T(8,128)}), f32[256,512]{1,0:T(8,128)}) %all-reduce.6.cloned.1.call-update) | async-done | bytes 524304 | tf_op jit(solution)/shard_map/psum | solution.py:36
  624.3 2.3 gather_fusion.5
  626.6 106.6 %all-gather.17.cloned.1.call-done = f32[8192,512]{1,0:T(8,128)} async-done(((f32[256,512]{1,0:T(8,128)}), f32[8192,512]{1,0:T(8,128)}) %all-gather.17.cloned.1.call-update) | async-done | bytes 16777232 | tf_op jit(solution)/shard_map/all_gather | solution.py:9
  733.2 7.8 reduce_sum.91
  740.9 1.0 gather_fusion.3
  742.0 1.1 fusion.4
  743.5 64.1 %all-gather.19.cloned.1.call-done = f32[4096,256]{1,0:T(8,128)} async-done(((f32[256,256]{1,0:T(8,128)}), f32[4096,256]{1,0:T(8,128)}) %all-gather.19.cloned.1.call-update) | async-done | bytes 4194320 | tf_op jit(solution)/shard_map/all_gather | solution.py:9
  807.6 2.5 reduce_sum.94
  810.8 1.5 broadcast_select_fusion.1
  812.2 1.0 gather_fusion.7
  813.2 0.9 broadcast_select_fusion
  815.0 207.1 %all-reduce.8.cloned.1.call-done = f32[256,512]{1,0:T(8,128)} async-done(((f32[256,512]{1,0:T(8,128)}), f32[256,512]{1,0:T(8,128)}) %all-reduce.8.cloned.1.call-update) | async-done | bytes 524304 | tf_op jit(solution)/shard_map/psum | solution.py:36
  1022.1 2.3 gather_fusion.8
  1024.4 106.9 %all-gather.21.cloned.1.call-done = f32[8192,512]{1,0:T(8,128)} async-done(((f32[256,512]{1,0:T(8,128)}), f32[8192,512]{1,0:T(8,128)}) %all-gather.21.cloned.1.call-update) | async-done | bytes 16777232 | tf_op jit(solution)/shard_map/all_gather | solution.py:9
  1131.3 7.8 reduce_sum.95
  1139.1 1.0 gather_fusion.6
  1140.2 1.1 fusion.3
  1141.4 64.4 %all-gather.23.cloned.1.call-done = f32[4096,256]{1,0:T(8,128)} async-done(((f32[256,256]{1,0:T(8,128)}), f32[4096,256]{1,0:T(8,128)}) %all-gather.23.cloned.1.call-update) | async-done | bytes 4194320 | tf_op jit(solution)/shard_map/all_gather | solution.py:9
  1205.8 2.5 reduce_sum.98
  1208.9 1.4 fusion
  (67 shorter events, 10.0 us)
Async XLA Ops:
  6.5 219.6 %all-reduce.4.cloned.1.call-start = ((), (), s32[]{:S(2)}) async-start(), calls=%async_computation | async-start | bytes 1048576 | tf_op jit(solution)/shard_map/psum | solution.py:36
  9.4 334.7 %copy-start = (f32[256,512]{1,0:T(8,128)S(1)}, f32[256,512]{1,0:T(8,128)}, u32[]{:S(2)}) copy-start(f32[256,512]{1,0:T(8,128)} %param.9) | copy-start | bytes 1572868
  11.7 332.5 %copy-start.4 = (f32[3,256,256]{2,1,0:T(8,128)S(1)}, f32[3,256,256]{2,1,0:T(8,128)}, u32[]{:S(2)}) copy-start(f32[3,256,256]{2,1,0:T(8,128)} %param.11) | copy-start | bytes 2359300
  12.7 322.7 %all-gather.13.cloned.1.call-start = ((), (), s32[]{:S(2)}) async-start(), calls=%async_computation.3 | async-start | bytes 17301504 | tf_op jit(solution)/shard_map/all_gather | solution.py:9
  13.6 396.2 %all-gather.15.cloned.1.call-start = ((), (), s32[]{:S(2)}) async-start(), calls=%async_computation.4 | async-start | bytes 4456448 | tf_op jit(solution)/shard_map/all_gather | solution.py:9
  226.1 186.9 %copy-start.1 = (f32[256,512]{1,0:T(8,128)S(1)}, f32[256,512]{1,0:T(8,128)}, u32[]{:S(2)}) copy-start(f32[256,512]{1,0:T(8,128)} %all-reduce.4.cloned.1.call-done) | copy-start | bytes 1572868
  345.4 278.9 %all-reduce.6.cloned.1.call-start = ((), (), s32[]{:S(2)}) async-start(), calls=%async_computation.1 | async-start | bytes 1048576 | tf_op jit(solution)/shard_map/psum | solution.py:36
  416.4 316.8 %all-gather.17.cloned.1.call-start = ((), (), s32[]{:S(2)}) async-start(), calls=%async_computation.5 | async-start | bytes 17301504 | tf_op jit(solution)/shard_map/all_gather | solution.py:9
  416.9 390.7 %all-gather.19.cloned.1.call-start = ((), (), s32[]{:S(2)}) async-start(), calls=%async_computation.6 | async-start | bytes 4456448 | tf_op jit(solution)/shard_map/all_gather | solution.py:9
  624.3 186.5 %copy-start.2 = (f32[256,512]{1,0:T(8,128)S(1)}, f32[256,512]{1,0:T(8,128)}, u32[]{:S(2)}) copy-start(f32[256,512]{1,0:T(8,128)} %all-reduce.6.cloned.1.call-done) | copy-start | bytes 1572868
  743.2 278.9 %all-reduce.8.cloned.1.call-start = ((), (), s32[]{:S(2)}) async-start(), calls=%async_computation.2 | async-start | bytes 1048576 | tf_op jit(solution)/shard_map/psum | solution.py:36
  814.1 317.2 %all-gather.21.cloned.1.call-start = ((), (), s32[]{:S(2)}) async-start(), calls=%async_computation.7 | async-start | bytes 17301504 | tf_op jit(solution)/shard_map/all_gather | solution.py:9
  814.9 390.9 %all-gather.23.cloned.1.call-start = ((), (), s32[]{:S(2)}) async-start(), calls=%async_computation.8 | async-start | bytes 4456448 | tf_op jit(solution)/shard_map/all_gather | solution.py:9
  1022.1 186.9 %copy-start.3 = (f32[256,512]{1,0:T(8,128)S(1)}, f32[256,512]{1,0:T(8,128)}, u32[]{:S(2)}) copy-start(f32[256,512]{1,0:T(8,128)} %all-reduce.8.cloned.1.call-done) | copy-start | bytes 1572868
Sparse Core Ops, SparseCore 0:
  12.8 213.2 all-reduce.3
  228.4 106.8 all-gather.12
  345.5 64.2 all-gather.14
  416.5 207.7 all-reduce.5
  626.2 106.8 all-gather.16
  743.3 64.2 all-gather.18
  814.3 207.7 all-reduce.7
  1024.4 106.8 all-gather.20
  1141.4 64.2 all-gather.22
